TPU v7x, 32 devices: a whole 2x2x4 slice. The times are simulated.
32 devices in a mesh: row: 8 (over y, x, core), col: 4 (over z).
Axes of the slice: x: 2, y: 2, z: 4, core: 2. Of those that a mesh axis runs over, the one named last changes fastest.
Arguments:
- child_tiles: float32 [896, 256, 128], P(('row', 'col')), may hold values from -2.5 to 2.5
- tile_dest: int32 [896], P(('row', 'col')), may hold values from 0 to 3071, as said below
- tile_mask: int32 [896, 256], P(('row', 'col')), may hold values 0 or 1
- tile_count: int32 [32], P(('row', 'col')), may hold values from 21 to 28, as said below
- front_diagonal: float32 [2, 1024], P(None, 'col'), may hold values from 200 to 400
Outputs:
- front_out: float32 [49152, 2, 1024], P('row', None, 'col')
Inputs may be any that keep to these rules, and one draw needn't show every extreme that they name: tile_dest[i] = r * 16 + t names front rows r * 256 onward and slab columns t * 128 onward; of the 28 tiles of one device at most 2 name tiles that lie on any one device of front_out's placement, and that most is reached. Tile i * 28 + m is live when m < tile_count[i].
All inputs are finite; a program needn't handle non-finite values. No bound on the sum of `tile_mask` on one device may be relied on, other than what follows from the above.
Results may differ from a plain program's by a relative error of at most 0.0001.
Values sent between devices are 32-bit elements; how exact they have to be, the bound alone decides.
A program may use at most 192 MiB of HBM per device.

v0:
```python
import jax
import jax.numpy as jnp
from jax import lax
from jax.sharding import PartitionSpec as P

NF = 49152
CAP = 2


def from_root(x, axis, root):
    mine = lax.axis_index(axis) == root
    return lax.psum(jnp.where(mine, x, jnp.zeros_like(x)), axis)


def factor_panel(front_local, section, rows_global, cols_global, row_index, col_index):
    local_rows, col_blocks, panel_width = front_local.shape
    n_col = lax.axis_size("col")
    lower_edge = section * panel_width
    upper_edge = lower_edge + panel_width
    owner_col = section % n_col
    owner_block = section // n_col
    owner_row = lower_edge // local_rows
    start_row = lower_edge - owner_row * local_rows
    column = front_local[:, owner_block, :]
    diag_piece = lax.slice_in_dim(column, start_row, start_row + panel_width, axis=0)
    is_root = jnp.logical_and(row_index == owner_row, col_index == owner_col)
    diag_piece = jnp.where(is_root, diag_piece, jnp.eye(panel_width, dtype=jnp.float32))
    pivot = from_root(diag_piece, ("row", "col"), owner_row * n_col + owner_col)
    factor = jnp.linalg.cholesky(0.5 * (pivot + pivot.T))
    panel_raw = from_root(column, "col", owner_col)
    solved = jax.scipy.linalg.solve_triangular(factor, panel_raw.T, lower=True).T
    inner_row = jnp.clip(rows_global - lower_edge, 0, panel_width - 1)
    factor_rows = factor[inner_row]
    row_column = rows_global[:, None]
    lower_panel = jnp.where(
        row_column < lower_edge,
        jnp.zeros_like(solved),
        jnp.where(row_column < upper_edge, factor_rows, solved),
    )
    offset = cols_global - row_index * local_rows
    inside = jnp.logical_and(offset >= 0, offset < local_rows)
    picked = lower_panel[jnp.clip(offset, 0, local_rows - 1)] * inside[:, :, None].astype(
        jnp.float32
    )
    panel_rows = lax.psum(picked, "row")
    return (lower_panel, panel_rows)


def advance(front_part, lower_panel, panel_rows, section, cols_part):
    local_rows, col_blocks, panel_width = front_part.shape
    product = jnp.dot(
        lower_panel, panel_rows.reshape(-1, panel_width).T, precision=lax.Precision.HIGHEST
    ).reshape(local_rows, col_blocks, panel_width)
    upper_edge = (section + 1) * panel_width
    trailing = (cols_part >= upper_edge)[None, :, :]
    own_block = (cols_part // panel_width == section)[None, :, :]
    return jnp.where(
        trailing, front_part - product, jnp.where(own_block, lower_panel[:, None, :], front_part)
    )


def on_device(child_tiles, tile_dest, tile_mask, tile_count, front_diagonal):
    n_row = lax.axis_size("row")
    n_col = lax.axis_size("col")
    devices = n_row * n_col
    row_index = lax.axis_index("row")
    col_index = lax.axis_index("col")
    tile_total, tile_rows, tile_cols = child_tiles.shape
    col_blocks, panel_width = front_diagonal.shape
    halves = panel_width // tile_cols
    local_rows = NF // n_row
    row_tiles = local_rows // tile_rows
    col_tiles = col_blocks * n_col * halves
    is_live = jnp.arange(tile_total, dtype=jnp.int32) < tile_count[0]
    row_tile = tile_dest // col_tiles
    col_tile = tile_dest % col_tiles
    col_block = col_tile // halves
    col_half = col_tile % halves
    owner_row = row_tile // row_tiles
    owner_dev = jnp.where(is_live, owner_row * n_col + col_block % n_col, devices)
    onehot = (owner_dev[:, None] == jnp.arange(devices, dtype=jnp.int32)[None, :]).astype(jnp.int32)
    slot_rank = jnp.sum((jnp.cumsum(onehot, axis=0) - onehot) * onehot, axis=1)
    position = jnp.where(is_live, owner_dev * CAP + slot_rank, devices * CAP)
    local_tile = (
        (row_tile - owner_row * row_tiles) * (col_blocks * halves)
        + col_block // n_col * halves
        + col_half
    )
    masked = child_tiles * tile_mask.astype(jnp.float32)[:, :, None]
    outgoing = (
        jnp.zeros((devices * CAP + 1, tile_rows, tile_cols), jnp.float32)
        .at[position]
        .set(masked)[: devices * CAP]
    )
    targets = (
        jnp.full((devices * CAP + 1,), -1, jnp.int32).at[position].set(local_tile)[: devices * CAP]
    )
    arrived, arrived_targets = (
        lax.all_to_all(
            outgoing.reshape(devices, CAP, tile_rows, tile_cols),
            ("row", "col"),
            split_axis=0,
            concat_axis=0,
            tiled=True,
        ),
        lax.all_to_all(
            targets.reshape(devices, CAP), ("row", "col"), split_axis=0, concat_axis=0, tiled=True
        ),
    )
    n_local = row_tiles * col_blocks * halves
    flat_targets = arrived_targets.reshape(-1)
    flat_targets = jnp.where(flat_targets < 0, n_local, flat_targets)
    summed = jax.ops.segment_sum(
        arrived.reshape(-1, tile_rows, tile_cols), flat_targets, num_segments=n_local + 1
    )[:n_local]
    front_local = summed.reshape(row_tiles, col_blocks, halves, tile_rows, tile_cols)
    front_local = front_local.transpose(0, 3, 1, 2, 4).reshape(local_rows, col_blocks, panel_width)
    cols_global = (
        jnp.arange(col_blocks, dtype=jnp.int32)[:, None] * n_col + col_index
    ) * panel_width + jnp.arange(panel_width, dtype=jnp.int32)[None, :]
    rows_global = row_index * local_rows + jnp.arange(local_rows, dtype=jnp.int32)
    offset = cols_global - row_index * local_rows
    inside = jnp.logical_and(offset >= 0, offset < local_rows)
    block_ids = jnp.broadcast_to(
        jnp.arange(col_blocks, dtype=jnp.int32)[:, None], (col_blocks, panel_width)
    )
    lane_ids = jnp.broadcast_to(
        jnp.arange(panel_width, dtype=jnp.int32)[None, :], (col_blocks, panel_width)
    )
    front_local = front_local.at[jnp.clip(offset, 0, local_rows - 1), block_ids, lane_ids].add(
        jnp.where(inside, front_diagonal, jnp.zeros_like(front_diagonal))
    )
    for section in range(2):
        lower_panel, panel_rows = factor_panel(
            front_local, section, rows_global, cols_global, row_index, col_index
        )
        front_local = advance(front_local, lower_panel, panel_rows, section, cols_global)
    return front_local


def solution(mesh):
    in_specs = (
        P(("row", "col"), None, None),
        P(("row", "col")),
        P(("row", "col"), None),
        P(("row", "col")),
        P(None, "col"),
    )
    out_specs = P("row", None, "col")
    return jax.shard_map(
        on_device, mesh=mesh, in_specs=in_specs, out_specs=out_specs, check_vma=False
    )
```

profile of v0, /device:TPU:24, one launch (start us, length us, event | category | flops | bytes accessed | tf_op | source)
XLA Modules:
  0.0 1353.6 jit_solution(16987304984082663930)
XLA Ops:
  10.2 5.9 all-to-all-start
  20.8 4.5 broadcast_in_dim.129
  25.3 8.0 scatter_fusion
  33.3 7.6 slice.95
  40.9 6.0 all-to-all-start.1
  48.5 176.2 %all-to-all-done.1 = f32[32,2,256,128]{3,2,1,0:T(8,128)} async-done(((f32[32,2,256,128]{3,2,1,0:T(8,128)}), f32[32,2,256,128]{3,2,1,0:T(8,128)}, u32[]{:S(2)}, u32[]{:S(2)}) %all-to-all-start.1) | async-done | bytes 8388640 | tf_op jit(solution)/shard_map/all_to_all | solution.py:99
  224.7 6.1 broadcast_in_dim.123
  230.8 18.8 %scatter_fusion.1 = f32[97,256,128]{2,1,0:T(8,128)} fusion(f32[97,256,128]{2,1,0:T(8,128)} %broadcast_in_dim.123, s32[64]{0:T(128)S(1)} %fusion.43, f32[64,256,128]{2,1,0:T(8,128)} %bitcast.4), kind=kCustom, calls=%fused_computation.6 | custom fusion | flops 2097152 | bytes 25166080 | tf_op jit(solution)/shard_map/scatter-add | solution.py:113
  249.6 10.9 slice.96
  260.6 22.0 %copy.32 = f32[24,256,2,2,128]{4,3,1,0,2:T(2,128)} copy(f32[24,256,2,2,128]{4,1,3,2,0:T(8,128)} %bitcast.133) | data formatting | bytes 25165824 | tf_op jit(solution)/shard_map/transpose | solution.py:117
  282.6 16.5 %reshape.313 = f32[6144,2,256]{2,0,1:T(8,128)} reshape(f32[24,256,2,2,128]{4,3,1,0,2:T(2,128)} %copy.32) | data formatting | bytes 25165824 | tf_op jit(solution)/shard_map/reshape | solution.py:117
  299.1 74.1 %scatter_fusion.2 = f32[6144,2,256]{2,0,1:T(8,128)} fusion(f32[6144,2,256]{2,0,1:T(8,128)} %reshape.313, s32[512]{0:T(512)S(1)} %bitcast.134, f32[512]{0:T(512)S(1)} %bitcast.144), kind=kCustom, calls=%fused_computation.7 | custom fusion | flops 512 | bytes 12288 | tf_op jit(solution)/shard_map/scatter-add | solution.py:130
  374.9 5.8 fusion.1
  381.3 134.0 %all-reduce.8.cloned.1.call-done = f32[256,256]{1,0:T(8,128)} async-done(((f32[256,256]{1,0:T(8,128)}), f32[256,256]{1,0:T(8,128)}) %all-reduce.8.cloned.1.call-update) | async-done | bytes 262160 | tf_op jit(solution)/shard_map/psum | solution.py:12
  517.6 11.7 cholesky.130
  529.3 9.8 custom-call.15
  539.6 11.7 cholesky.147
  553.5 4.0 while.4
  557.5 19.7 %custom-call.16 = f32[2,128,128]{1,2,0:T(8,128)S(1)} custom-call(f32[2,128,128]{2,1,0:T(8,128)S(1)} %get-tuple-element.21), custom_call_target="InvertDiagBlocksLowerTriangular" | custom-call | tf_op jit(solution)/shard_map/jit(_solve_triangular)/triangular_solve | solution.py:31
  577.2 23.7 %gather_fusion = f32[6144,256]{1,0:T(8,128)} fusion(f32[256,256]{1,0:T(8,128)S(1)} %get-tuple-element.42, s32[6144]{0:T(1024)S(1)} %broadcast_clamp_fusion.1), kind=kCustom, calls=%fused_computation | custom fusion | bytes 12607488 | tf_op jit(solution)/shard_map/gather | solution.py:33
  600.9 7.1 copy.36
  608.0 130.2 %all-reduce.10.cloned.1.call-done = f32[256,6144]{0,1:T(8,128)} async-done(((f32[256,6144]{0,1:T(8,128)}), f32[256,6144]{0,1:T(8,128)}) %all-reduce.10.cloned.1.call-update) | async-done | bytes 6291472 | tf_op jit(solution)/shard_map/psum | solution.py:12
  738.3 5.0 fusion.10
  743.3 7.4 convolution_subtract_fusion.1
  750.7 4.6 fusion.24
  755.4 6.0 fusion.3
  761.3 6.5 copy.37
  767.9 4.4 gather_fusion.1
  773.3 55.8 %all-reduce.12.cloned.1.call-done = f32[2,256,256]{2,1,0:T(8,128)} async-done(((f32[2,256,256]{2,1,0:T(8,128)}), f32[2,256,256]{2,1,0:T(8,128)}) %all-reduce.12.cloned.1.call-update) | async-done | bytes 524304 | tf_op jit(solution)/shard_map/psum | solution.py:45
  829.1 28.1 %select_select_fusion.1 = f32[6144,2,256]{2,0,1:T(8,128)} fusion(f32[6144,2,256]{2,0,1:T(8,128)} %scatter_fusion.2, f32[2,256,256]{2,1,0:T(8,128)} %all-reduce.12.cloned.1.call-done, f32[6144,256]{0,1:T(8,128)} %fusion.3, f32[6144,256]{1,0:T(8,128)} %copy.37, pred[2,256]{1,0:T(4,128)(4,1)S(1)} %get-tuple-element.63, pred[2,256]{1,0:T(4,128)(4,1)S(1)} %get-tuple-element.64), kind=kOutput, calls=%fused_computation.13 | convolution fusion | flops 9673113600 | bytes 38274048 | tf_op jit(solution)/shard_map/dot_general | solution.py:51
  859.4 5.8 fusion
  865.5 117.0 %all-reduce.14.cloned.1.call-done = f32[256,256]{1,0:T(8,128)} async-done(((f32[256,256]{1,0:T(8,128)}), f32[256,256]{1,0:T(8,128)}) %all-reduce.14.cloned.1.call-update) | async-done | bytes 262160 | tf_op jit(solution)/shard_map/psum | solution.py:12
  984.9 11.7 cholesky.164
  996.7 9.8 custom-call.17
  1007.0 11.7 cholesky.181
  1025.5 19.7 %custom-call.18 = f32[2,128,128]{1,2,0:T(8,128)S(1)} custom-call(f32[2,128,128]{2,1,0:T(8,128)S(1)} %get-tuple-element.22), custom_call_target="InvertDiagBlocksLowerTriangular" | custom-call | tf_op jit(solution)/shard_map/jit(_solve_triangular)/triangular_solve | solution.py:31
  1045.1 23.7 %gather_fusion.2 = f32[6144,256]{1,0:T(8,128)} fusion(f32[256,256]{1,0:T(8,128)S(1)} %get-tuple-element.40, s32[6144]{0:T(1024)S(1)} %broadcast_clamp_fusion), kind=kCustom, calls=%fused_computation.2 | custom fusion | bytes 12607488 | tf_op jit(solution)/shard_map/gather | solution.py:33
  1068.9 6.8 copy.43
  1075.6 129.8 %all-reduce.16.cloned.1.call-done = f32[256,6144]{0,1:T(8,128)} async-done(((f32[256,6144]{0,1:T(8,128)}), f32[256,6144]{0,1:T(8,128)}) %all-reduce.16.cloned.1.call-update) | async-done | bytes 6291472 | tf_op jit(solution)/shard_map/psum | solution.py:12
  1205.5 5.0 fusion.8
  1210.5 7.4 convolution_subtract_fusion
  1217.9 4.6 fusion.20
  1222.5 6.0 fusion.5
  1228.5 6.6 copy.44
  1235.0 4.4 gather_fusion.3
  1240.3 55.9 %all-reduce.18.cloned.1.call-done = f32[2,256,256]{2,1,0:T(8,128)} async-done(((f32[2,256,256]{2,1,0:T(8,128)}), f32[2,256,256]{2,1,0:T(8,128)}) %all-reduce.18.cloned.1.call-update) | async-done | bytes 524304 | tf_op jit(solution)/shard_map/psum | solution.py:45
  1296.2 28.1 %select_select_fusion = f32[6144,2,256]{2,0,1:T(8,128)} fusion(f32[6144,2,256]{2,0,1:T(8,128)} %select_select_fusion.1, f32[2,256,256]{2,1,0:T(8,128)} %all-reduce.18.cloned.1.call-done, f32[6144,256]{0,1:T(8,128)} %fusion.5, f32[6144,256]{1,0:T(8,128)} %copy.44, pred[2,256]{1,0:T(4,128)(4,1)S(1)} %get-tuple-element.62, ...), kind=kOutput, calls=%fused_computation.12 | convolution fusion | flops 9673113600 | bytes 38274048 | tf_op jit(solution)/shard_map/dot_general | solution.py:51
  1324.4 22.0 %copy.46 = f32[6144,2,256]{2,1,0:T(2,128)} copy(f32[6144,2,256]{2,0,1:T(8,128)} %select_select_fusion) | data formatting | bytes 25165824 | tf_op jit(solution)/shard_map/jit(_where)/select_n | solution.py:57
  (102 shorter events, 35.7 us)
Async XLA Ops:
  10.2 30.6 %all-to-all-start = ((s32[32,1,2]{2,1,0:T(1,128)}), s32[32,1,2]{2,1,0:T(1,128)S(1)}, u32[]{:S(2)}, u32[]{:S(2)}) async-start(s32[32,1,2]{2,1,0:T(1,128)} %bitcast.1), calls=%async_computation | async-start | bytes 32768 | tf_op jit(solution)/shard_map/all_to_all | solution.py:106
  40.9 6.2 copy-start
  40.9 183.8 %all-to-all-start.1 = ((f32[32,2,256,128]{3,2,1,0:T(8,128)}), f32[32,2,256,128]{3,2,1,0:T(8,128)}, u32[]{:S(2)}, u32[]{:S(2)}) async-start(f32[32,2,256,128]{3,2,1,0:T(8,128)} %bitcast.135), calls=%async_computation.1 | async-start | bytes 16777216 | tf_op jit(solution)/shard_map/all_to_all | solution.py:99
  46.9 468.4 %all-reduce.8.cloned.1.call-start = ((), (), s32[]{:S(2)}) async-start(), calls=%async_computation.2 | async-start | bytes 524288 | tf_op jit(solution)/shard_map/psum | solution.py:12
  374.9 363.4 %all-reduce.10.cloned.1.call-start = ((), (), s32[]{:S(2)}) async-start(), calls=%async_computation.3 | async-start | bytes 12582912 | tf_op jit(solution)/shard_map/psum | solution.py:12
  380.8 448.3 %all-reduce.12.cloned.1.call-start = ((), (), s32[]{:S(2)}) async-start(), calls=%async_computation.4 | async-start | bytes 1048576 | tf_op jit(solution)/shard_map/psum | solution.py:45
  738.3 17.1 %slice-start = ((s8[6291456]{0:T(1024)(128)(4,1)}), s8[4194304]{0:T(1024)(128)(4,1)S(1)}, s32[]{:S(2)}) async-start(s8[6291456]{0:T(1024)(128)(4,1)} %bitcast.136), calls=%async_computation.8 | async-start | bytes 8388608
  743.3 12.1 slice-start.1
  773.2 209.2 %all-reduce.14.cloned.1.call-start = ((), (), s32[]{:S(2)}) async-start(), calls=%async_computation.5 | async-start | bytes 524288 | tf_op jit(solution)/shard_map/psum | solution.py:12
  859.0 346.5 %all-reduce.16.cloned.1.call-start = ((), (), s32[]{:S(2)}) async-start(), calls=%async_computation.6 | async-start | bytes 12582912 | tf_op jit(solution)/shard_map/psum | solution.py:12
  865.3 430.9 %all-reduce.18.cloned.1.call-start = ((), (), s32[]{:S(2)}) async-start(), calls=%async_computation.7 | async-start | bytes 1048576 | tf_op jit(solution)/shard_map/psum | solution.py:45
  1205.5 17.1 %slice-start.2 = ((s8[6291456]{0:T(1024)(128)(4,1)}), s8[4194304]{0:T(1024)(128)(4,1)S(1)}, s32[]{:S(2)}) async-start(s8[6291456]{0:T(1024)(128)(4,1)} %bitcast.138), calls=%async_computation.10 | async-start | bytes 8388608
  1210.5 12.0 slice-start.3
Sparse Core Ops, SparseCore 0:
  375.0 140.2 all-reduce.7
  517.7 220.5 all-reduce.9
  773.3 55.7 all-reduce.11
  859.1 123.3 all-reduce.13
  984.8 220.6 all-reduce.15
  1240.5 55.7 all-reduce.17
where the time goes:
time: 1370 us; the launch traced here: 1350 us
  waiting for transfers between devices  799 us (58%)
  other arithmetic  239 us (17%)
  local copies, waits for them, and re-layouts  193 us (14%)
  matrix products  91.3 us (7%)
  between operations  17.5 us (1%)
    psum x4, waiting for transfers between devices, from_root(): return lax.psum(jnp.where(mine, x, jnp.zeros_like(x)), axis)  511 us
    all_to_all x1, waiting for transfers between devices, on_device(): lax.all_to_all(outgoing.reshape(devices, CAP, tile_rows, tile_cols), ('ro...  176 us
    psum x2, waiting for transfers between devices, factor_panel(): panel_rows = lax.psum(picked, 'row')  112 us
    scatter-add x1, other arithmetic, on_device(): front_local.at[jnp.clip(offset, 0, local_rows - 1), block_ids, lane_ids]  74.1 us
    another operation x13, other arithmetic, factor_panel(): factor = jnp.linalg.cholesky(0.5 * (pivot + pivot.T))  68.7 us
    gather x4, local copies, waits for them, and re-layouts, factor_panel(): factor_rows = factor[inner_row]  61.3 us
    dot_general x2, matrix products, advance(): jnp.dot(lower_panel, panel_rows.reshape(-1, panel_width).T, precision=lax...  56.3 us
    another operation x5, other arithmetic, factor_panel(): jax.scipy.linalg.solve_triangular(factor, panel_raw.T, lower=True)  39.4 us
  transfers between devices with their start and end apart: 8, of which 7 were waited for; matrix products, arithmetic and copies ran while one was open for 16% of the time, Pallas kernels for 0%

commit v1 on v0

v1 whole, which is shorter than its diff:
```python
import functools

import jax
import jax.numpy as jnp
from jax import lax
from jax.experimental import pallas as pl
from jax.experimental.pallas import tpu as pltpu
from jax.sharding import PartitionSpec as P

NF = 49152
CAP = 2
SECTIONS = 2
HI = lax.Precision.HIGHEST
MESH = pl.DeviceIdType.MESH


def mm(a, b):
    return jnp.dot(a, b, precision=HI)


def add_tiles(order_ref, start_ref, arrived_ref, position, shape):
    first = start_ref[position]
    last = start_ref[position + 1]
    return lax.fori_loop(
        first, last, lambda i, acc: acc + arrived_ref[order_ref[i]], jnp.zeros(shape, jnp.float32)
    )


def diagonal_tile(diag_row, half, shape):
    rows = lax.broadcasted_iota(jnp.int32, shape, 0)
    cols = lax.broadcasted_iota(jnp.int32, shape, 1) + half * shape[1]
    return jnp.where(rows == cols, diag_row, 0.0)


def panel_kernel(halves, order_ref, start_ref, where_ref, arrived_ref, diag_ref, out_ref):
    step = pl.program_id(0)
    shape = out_ref.shape[2:]
    base = where_ref[0] + step

    @pl.when(where_ref[1] < SECTIONS)
    def _():
        for half in range(halves):
            out_ref[0, half] = add_tiles(
                order_ref, start_ref, arrived_ref, step * where_ref[2] + half, shape
            )

        @pl.when(base == where_ref[1])
        def _():
            for half in range(halves):
                diag_row = diag_ref[0:1, half * shape[1] : (half + 1) * shape[1]]
                out_ref[0, half] += diagonal_tile(diag_row, half, shape)


def chain_kernel(n_row, n_col, col_blocks, pieces, own_ref, all_ref, rows_ref, copy_sem, send_sem, recv_sem, rsend_sem, rrecv_sem):
    row = lax.axis_index("row")
    col = lax.axis_index("col")
    row_tiles = own_ref.shape[0]
    per = row_tiles // pieces
    barrier = pltpu.get_barrier_semaphore()
    for step in (1, -1):
        inside = (col < n_col - 1) if step == 1 else (col > 0)

        @pl.when(inside)
        def _():
            pl.semaphore_signal(
                barrier, inc=1, device_id={"col": col + step}, device_id_type=MESH
            )

    for shift in range(1, n_row):
        pl.semaphore_signal(
            barrier,
            inc=1,
            device_id={"row": lax.rem(row + shift, n_row)},
            device_id_type=MESH,
        )

    at_end = jnp.logical_or(col == 0, col == n_col - 1)

    @pl.when(at_end)
    def _():
        pl.semaphore_wait(barrier, n_row)

    @pl.when(jnp.logical_not(at_end))
    def _():
        pl.semaphore_wait(barrier, n_row + 1)

    def part(ref, piece):
        return ref.at[pl.ds(piece * per, per)]

    def hop(section, piece, step, from_own):
        target = all_ref.at[section]
        source = own_ref if from_own else target
        way = 0 if step == 1 else 1
        return pltpu.make_async_remote_copy(
            src_ref=part(source, piece),
            dst_ref=part(target, piece),
            send_sem=send_sem.at[section, way, piece],
            recv_sem=recv_sem.at[section, piece],
            device_id={"col": col + step},
            device_id_type=MESH,
        )

    def local(section):
        return pltpu.make_async_copy(own_ref, all_ref.at[section], copy_sem)

    for section in range(SECTIONS):

        @pl.when(col == section)
        def _():
            local(section).start()
            for piece in range(pieces):
                hop(section, piece, 1, True).start()
                if section > 0:
                    hop(section, piece, -1, True).start()
            local(section).wait()

    def row_copy(block, section, shift):
        tile = block * n_col + col
        return pltpu.make_async_remote_copy(
            src_ref=all_ref.at[section, lax.rem(tile, row_tiles)],
            dst_ref=rows_ref.at[block, section],
            send_sem=rsend_sem.at[block, section, shift],
            recv_sem=rrecv_sem.at[block, section],
            device_id={"row": lax.rem(row + shift, n_row)},
            device_id_type=MESH,
        )

    def row_local(block, section):
        tile = block * n_col + col
        return pltpu.make_async_copy(
            all_ref.at[section, lax.rem(tile, row_tiles)],
            rows_ref.at[block, section],
            rsend_sem.at[block, section, 0],
        )

    def owner(block):
        return row == (block * n_col + col) // row_tiles

    needed = min(col_blocks * n_col, row_tiles)
    send_rows_at = -(-needed // per) - 1
    for piece in range(pieces):
        for section in range(SECTIONS):

            @pl.when(col != section)
            def _():
                hop(section, piece, 1, False).wait_recv()

            if section < n_col - 1:

                @pl.when(jnp.logical_and(col > section, col < n_col - 1))
                def _():
                    hop(section, piece, 1, False).start()

            if section > 1:

                @pl.when(jnp.logical_and(col < section, col > 0))
                def _():
                    hop(section, piece, -1, False).start()

        if piece == send_rows_at:
            for block in range(col_blocks):

                @pl.when(owner(block))
                def _():
                    for section in range(SECTIONS):
                        for shift in range(1, n_row):
                            row_copy(block, section, shift).start()
                        row_local(block, section).start()

    for block in range(col_blocks):

        @pl.when(owner(block))
        def _():
            for section in range(SECTIONS):
                for shift in range(1, n_row):
                    row_copy(block, section, shift).wait_send()
                row_local(block, section).wait()

        @pl.when(jnp.logical_not(owner(block)))
        def _():
            for section in range(SECTIONS):
                row_copy(block, section, 1).wait_recv()

    for section in range(SECTIONS):
        for piece in range(pieces):

            @pl.when(jnp.logical_and(col >= section, col < n_col - 1))
            def _():
                hop(section, piece, 1, False).wait_send()

            if section > 0:

                @pl.when(jnp.logical_and(col <= section, col > 0))
                def _():
                    hop(section, piece, -1, False).wait_send()


def final_kernel(col_blocks, halves, n_col, order_ref, start_ref, where_ref, arrived_ref, diag_ref, panels_ref, whi_ref, wlo_ref, top_ref, own_ref, out_ref, lhs_ref):
    step = pl.program_id(0)
    rows, lanes = arrived_ref.shape[1:]
    width = halves * lanes
    base = where_ref[0] + step
    for section in range(SECTIONS):
        for half in range(halves):
            low = section * width + half * lanes
            lhs_ref[:, low : low + lanes] = panels_ref[section, 0, half]

    @pl.when(base < SECTIONS)
    def _():
        lhs_ref[...] = top_ref[jnp.minimum(base, SECTIONS - 1)]

    lhs = lhs_ref[...]
    hi = lhs.astype(jnp.bfloat16)
    lo = (lhs - hi.astype(jnp.float32)).astype(jnp.bfloat16)
    whi = whi_ref[...]
    product = (
        jnp.dot(hi, wlo_ref[...], preferred_element_type=jnp.float32)
        + jnp.dot(lo, whi, preferred_element_type=jnp.float32)
    ) + jnp.dot(hi, whi, preferred_element_type=jnp.float32)
    panel_column = where_ref[1] < SECTIONS
    group = col_blocks * halves
    for block in range(col_blocks):
        for half in range(halves):
            low = block * width + half * lanes
            value = product[:, low : low + lanes]
            slot = half * col_blocks + block
            place = (pl.ds(slot, rows, stride=group), slice(None))

            def trailing():
                position = step * group + block * halves + half
                out_ref[place] = value + add_tiles(
                    order_ref, start_ref, arrived_ref, position, (rows, lanes)
                )

                @pl.when(base == block * n_col + where_ref[1])
                def _():
                    diag_row = diag_ref[block : block + 1, half * lanes : (half + 1) * lanes]
                    out_ref[place] = out_ref[place] + diagonal_tile(diag_row, half, (rows, lanes))

            if block > 0:
                trailing()
            else:
                pl.when(jnp.logical_not(panel_column))(trailing)

                @pl.when(panel_column)
                def _():
                    out_ref[place] = value

                @pl.when(jnp.logical_and(panel_column, base < SECTIONS))
                def _():
                    out_ref[place] = own_ref[
                        jnp.minimum(base, SECTIONS - 1), :, half * lanes : (half + 1) * lanes
                    ]


def on_device(n_row, n_col, child_tiles, tile_dest, tile_mask, tile_count, front_diagonal):
    devices = n_row * n_col
    row_index = lax.axis_index("row")
    col_index = lax.axis_index("col")
    tile_total, tile_rows, tile_cols = child_tiles.shape
    col_blocks, panel_width = front_diagonal.shape
    halves = panel_width // tile_cols
    local_rows = NF // n_row
    row_tiles = local_rows // tile_rows
    col_tiles = col_blocks * n_col * halves
    is_live = jnp.arange(tile_total, dtype=jnp.int32) < tile_count[0]
    row_tile = tile_dest // col_tiles
    col_tile = tile_dest % col_tiles
    col_block = col_tile // halves
    col_half = col_tile % halves
    owner_row = row_tile // row_tiles
    owner_dev = jnp.where(is_live, owner_row * n_col + col_block % n_col, devices)
    local_tile = (
        (row_tile - owner_row * row_tiles) * (col_blocks * halves)
        + col_block // n_col * halves
        + col_half
    )
    earlier = jnp.tril(jnp.ones((tile_total, tile_total), jnp.int32), -1)
    slot_rank = jnp.sum((owner_dev[:, None] == owner_dev[None, :]) * earlier, axis=1)
    position = jnp.where(is_live, owner_dev * CAP + slot_rank, devices * CAP)
    hit = position[None, :] == jnp.arange(devices * CAP, dtype=jnp.int32)[:, None]
    source = jnp.sum(
        hit * jnp.arange(tile_total, dtype=jnp.int32)[None, :], axis=1, dtype=jnp.int32
    )
    targets = jnp.sum(hit * (local_tile + 1)[None, :], axis=1, dtype=jnp.int32) - 1
    masked = child_tiles * tile_mask.astype(jnp.float32)[:, :, None]
    outgoing = masked[source]
    arrived_targets = lax.all_to_all(
        targets.reshape(devices, CAP), ("row", "col"), split_axis=0, concat_axis=0, tiled=True
    )
    arrived = lax.all_to_all(
        outgoing.reshape(devices, CAP, tile_rows, tile_cols),
        ("row", "col"),
        split_axis=0,
        concat_axis=0,
        tiled=True,
    ).reshape(-1, tile_rows, tile_cols)

    wide = SECTIONS * panel_width
    pivot_tiles = SECTIONS * halves
    in_pivot = is_live & (row_tile < SECTIONS) & (col_tile < pivot_tiles)
    pivot_slot = jnp.where(in_pivot, row_tile * pivot_tiles + col_tile, SECTIONS * pivot_tiles)
    pivot = jax.ops.segment_sum(masked, pivot_slot, num_segments=SECTIONS * pivot_tiles + 1)
    pivot = lax.psum(pivot[: SECTIONS * pivot_tiles], ("row", "col"))
    pivot = pivot.reshape(SECTIONS, pivot_tiles, tile_rows, tile_cols)
    pivot = pivot.transpose(0, 2, 1, 3).reshape(wide, wide)
    one_col = (jnp.arange(SECTIONS, dtype=jnp.int32) == col_index)[:, None] & (row_index == 0)
    diag = lax.psum(jnp.where(one_col, front_diagonal[0][None, :], 0.0), ("row", "col"))
    pivot = pivot + jnp.diag(diag.reshape(-1))
    eye = jnp.eye(panel_width, dtype=jnp.float32)
    b00 = pivot[:panel_width, :panel_width]
    b10 = pivot[panel_width:, :panel_width]
    b11 = pivot[panel_width:, panel_width:]
    b00 = 0.5 * (b00 + b00.T)
    b11 = 0.5 * (b11 + b11.T)
    l00 = jnp.linalg.cholesky(b00)
    x0 = jax.scipy.linalg.solve_triangular(l00, eye, lower=True)
    l10 = mm(b10, x0.T)
    l11 = jnp.linalg.cholesky(b11 - mm(l10, l10.T))
    x1 = jax.scipy.linalg.solve_triangular(l11, eye, lower=True)
    zero = jnp.zeros_like(eye)
    inverse = jnp.block([[x0, zero], [-mm(x1, mm(l10, x0)), x1]])
    full = jnp.block([[l00, zero], [l10, l11]])
    top = jnp.block([[b00, b10.T], [b10, b11]]).reshape(SECTIONS, tile_rows, wide)
    gram = mm(inverse.T, inverse)
    section_at = jnp.minimum(col_index, SECTIONS - 1) * panel_width
    own_top = lax.dynamic_slice_in_dim(full, section_at, panel_width, axis=1)
    own_top = own_top.reshape(SECTIONS, tile_rows, panel_width)
    own_weight = lax.dynamic_slice_in_dim(inverse, section_at, panel_width, axis=0).T

    n_local = row_tiles * col_blocks * halves
    flat = arrived_targets.reshape(-1)
    flat = jnp.where(flat < 0, n_local, flat)
    slots = flat.shape[0]
    ids = jnp.arange(slots, dtype=jnp.int32)
    before = (flat[None, :] < flat[:, None]) | (
        (flat[None, :] == flat[:, None]) & (ids[None, :] < ids[:, None])
    )
    rank = jnp.sum(before, axis=1, dtype=jnp.int32)
    order = jnp.sum((rank[None, :] == ids[:, None]) * ids[None, :], axis=1, dtype=jnp.int32)
    start = jnp.sum(
        flat[None, :] < jnp.arange(n_local + 1, dtype=jnp.int32)[:, None], axis=1, dtype=jnp.int32
    )
    where = jnp.stack(
        [row_index * row_tiles, col_index, jnp.full((), col_blocks * halves, jnp.int32)]
    ).astype(jnp.int32)

    whole = pl.BlockSpec(memory_space=pltpu.VMEM)
    own_panel = pl.pallas_call(
        functools.partial(panel_kernel, halves),
        out_shape=jax.ShapeDtypeStruct((row_tiles, halves, tile_rows, tile_cols), jnp.float32),
        grid_spec=pltpu.PrefetchScalarGridSpec(
            num_scalar_prefetch=3,
            grid=(row_tiles,),
            in_specs=[whole, whole],
            out_specs=pl.BlockSpec(
                (1, halves, tile_rows, tile_cols), lambda t, *_: (t, 0, 0, 0)
            ),
        ),
        compiler_params=pltpu.CompilerParams(vmem_limit_bytes=52 * 2**20),
    )(order, start, where, arrived, front_diagonal)

    pieces = 12
    anywhere = pl.BlockSpec(memory_space=pl.ANY)
    panels, rows = pl.pallas_call(
        functools.partial(chain_kernel, n_row, n_col, col_blocks, pieces),
        out_shape=(
            jax.ShapeDtypeStruct(
                (SECTIONS, row_tiles, halves, tile_rows, tile_cols), jnp.float32
            ),
            jax.ShapeDtypeStruct(
                (col_blocks, SECTIONS, halves, tile_rows, tile_cols), jnp.float32
            ),
        ),
        in_specs=[anywhere],
        out_specs=(anywhere, anywhere),
        scratch_shapes=[
            pltpu.SemaphoreType.DMA,
            pltpu.SemaphoreType.DMA((SECTIONS, 2, pieces)),
            pltpu.SemaphoreType.DMA((SECTIONS, pieces)),
            pltpu.SemaphoreType.DMA((col_blocks, SECTIONS, n_row)),
            pltpu.SemaphoreType.DMA((col_blocks, SECTIONS)),
        ],
        compiler_params=pltpu.CompilerParams(collective_id=0, has_side_effects=True),
    )(own_panel)

    rows = rows.transpose(0, 3, 1, 2, 4).reshape(col_blocks * panel_width, wide)
    weight = -mm(gram, rows.T)
    first = jnp.where(col_index < SECTIONS, own_weight, weight[:, :panel_width])
    weight = jnp.concatenate([first, weight[:, panel_width:]], axis=1)
    weight_hi = weight.astype(jnp.bfloat16)
    weight_lo = (weight - weight_hi.astype(jnp.float32)).astype(jnp.bfloat16)

    group = col_blocks * halves
    out = pl.pallas_call(
        functools.partial(final_kernel, col_blocks, halves, n_col),
        out_shape=jax.ShapeDtypeStruct((local_rows * group, tile_cols), jnp.float32),
        grid_spec=pltpu.PrefetchScalarGridSpec(
            num_scalar_prefetch=3,
            grid=(row_tiles,),
            in_specs=[
                whole,
                whole,
                pl.BlockSpec(
                    (SECTIONS, 1, halves, tile_rows, tile_cols), lambda t, *_: (0, t, 0, 0, 0)
                ),
                whole,
                whole,
                whole,
                whole,
            ],
            out_specs=pl.BlockSpec((tile_rows * group, tile_cols), lambda t, *_: (t, 0)),
            scratch_shapes=[pltpu.VMEM((tile_rows, wide), jnp.float32)],
        ),
        compiler_params=pltpu.CompilerParams(vmem_limit_bytes=52 * 2**20),
    )(order, start, where, arrived, front_diagonal, panels, weight_hi, weight_lo, top, own_top)
    out = out.reshape(local_rows, halves, col_blocks, tile_cols).transpose(0, 2, 1, 3)
    return out.reshape(local_rows, col_blocks, panel_width)


def solution(mesh):
    in_specs = (
        P(("row", "col"), None, None),
        P(("row", "col")),
        P(("row", "col"), None),
        P(("row", "col")),
        P(None, "col"),
    )
    out_specs = P("row", None, "col")
    return jax.shard_map(
        functools.partial(on_device, mesh.shape["row"], mesh.shape["col"]),
        mesh=mesh,
        in_specs=in_specs,
        out_specs=out_specs,
        check_vma=False,
    )
```

time: 1370 us -> 943 us (0.69)
  waiting for transfers between devices: 799 us -> 17.5 us
  Pallas kernels: 0 us -> 522 us
  blocking collectives: 0 us -> 204 us
  local copies, waits for them, and re-layouts: 193 us -> 24.3 us
  other arithmetic: 239 us -> 130 us
  matrix products: 91.3 us -> 11.3 us
    psum x6 -> x1, waiting for transfers between devices: 623 us -> 17.5 us  [on_device(): pivot = lax.psum(pivot[:SECTIONS * pivot_tiles], ('row', 'col'))]
    pallas_call x0 -> x3, Pallas kernels: none -> 522 us  [the longest x1 480 us: on_device(): pl.pallas_call(functools.partial(chain_kernel, n_row, n_col, col_blocks,...]
    psum x0 -> x1, blocking collectives: none -> 204 us  [on_device(): lax.psum(jnp.where(one_col, front_diagonal[0][None, :], 0.0), ('row', 'co...]
    all_to_all x1, waiting for transfers between devices: 176 us -> 0.01 us  [on_device(): lax.all_to_all(outgoing.reshape(devices, CAP, tile_rows, tile_cols), ('ro...]
    scatter-add x2 -> x1, other arithmetic: 92.9 us -> 6.22 us  [on_device(): jax.ops.segment_sum(masked, pivot_slot, num_segments=SECTIONS * pivot_til...]
    gather x6 -> x1, local copies, waits for them, and re-layouts: 70 us -> 6.52 us  [on_device(): outgoing = masked[source]]
    dot_general x2 -> x6, matrix products: 56.3 us -> 8.28 us  [mm(): return jnp.dot(a, b, precision=HI)]
    select_n x3 -> x0, local copies, waits for them, and re-layouts: 35 us -> none  [the longest x1 22 us: advance(): jnp.where(trailing, front_part - product, jnp.where(own_block, lower_pane...]
  transfers between devices with their start and end apart: 8 -> 3, of which waited for: 7 -> 1; matrix products, arithmetic and copies ran while one was open for 16% -> 17% of each run, Pallas kernels for 0% -> 0%
where the time goes in v1:
time: 943 us; the launch traced here: 938 us
  Pallas kernels  522 us (55%)
  blocking collectives  204 us (22%)
  other arithmetic  130 us (14%)
  local copies, waits for them, and re-layouts  24.3 us (3%)
  waiting for transfers between devices  17.5 us (2%)
  between operations  17.2 us (2%)
  starting transfers between devices  11.8 us (1%)
  matrix products  11.3 us (1%)
    pallas_call x1, Pallas kernels, on_device(): pl.pallas_call(functools.partial(chain_kernel, n_row, n_col, col_blocks,...  480 us
    psum x1, blocking collectives, on_device(): lax.psum(jnp.where(one_col, front_diagonal[0][None, :], 0.0), ('row', 'co...  204 us
    another operation x7, other arithmetic, on_device(): l11 = jnp.linalg.cholesky(b11 - mm(l10, l10.T))  34.8 us
    another operation x6, other arithmetic, on_device(): l00 = jnp.linalg.cholesky(b00)  34 us
    pallas_call x1, Pallas kernels, on_device(): pl.pallas_call(functools.partial(final_kernel, col_blocks, halves, n_col)...  29.7 us
    another operation x4, other arithmetic, on_device(): x0 = jax.scipy.linalg.solve_triangular(l00, eye, lower=True)  20.8 us
    another operation x2, other arithmetic, on_device(): x1 = jax.scipy.linalg.solve_triangular(l11, eye, lower=True)  20.4 us
  transfers between devices with their start and end apart: 3, of which 1 were waited for; matrix products, arithmetic and copies ran while one was open for 17% of the time, Pallas kernels for 0%

profile of v1, /device:TPU:24, one launch (start us, length us, event | category | flops | bytes accessed | tf_op | source)
XLA Modules:
  0.0 938.2 jit_solution(8976821085241685150)
XLA Ops:
  7.2 0.7 and_select_fusion
  8.2 0.7 sub.34
  8.9 5.9 all-to-all-start
  14.8 0.8 convert_element_type.29
  15.6 3.9 broadcast_multiply_fusion
  19.5 6.5 gather_fusion
  26.0 5.9 all-to-all-start.1
  32.0 6.2 scatter_fusion
  38.3 0.7 copy.75
  39.0 1.1 copy.106
  40.3 203.8 %psum.15 = f32[512]{0:T(512)S(1)} all-reduce(f32[512]{0:T(512)S(1)} %bitcast.117), channel_id=1, replica_groups=mesh['row'=8,'col'=4] {'row','col'}, use_global_device_ids=true, to_apply=%region_8.9 | all-reduce | flops 512 | bytes 4096 | tf_op jit(solution)/shard_map/psum | solution.py:308
  245.9 17.5 %all-reduce.5.cloned.1.call-done = f32[512,512]{1,0:T(8,128)} async-done(((f32[512,512]{1,0:T(8,128)}), f32[512,512]{1,0:T(8,128)}) %all-reduce.5.cloned.1.call-update) | async-done | bytes 1048592 | tf_op jit(solution)/shard_map/psum | solution.py:304
  263.4 1.4 select_add_fusion
  265.1 0.8 slice_bitcast_fusion.8
  266.3 11.7 %cholesky.130 = f32[128,128]{1,0:T(8,128)S(1)} custom-call(f32[128,128]{1,0:T(8,128)S(1)} %copy.78), custom_call_target="Cholesky" | custom-call | tf_op jit(solution)/shard_map/jit(cholesky)/cholesky | solution.py:316
  278.1 9.8 %custom-call.13 = f32[1,128,128]{1,2,0:T(8,128)S(1)} custom-call(f32[1,128,128]{2,1,0:T(8,128)S(1)} %get-tuple-element.74), custom_call_target="InvertDiagBlocksLowerTriangular" | custom-call | tf_op jit(solution)/shard_map/jit(cholesky)/cholesky | solution.py:316
  288.6 11.7 %cholesky.147 = f32[128,128]{1,0:T(8,128)S(1)} custom-call(f32[128,128]{1,0:T(8,128)S(1)} %copy.80), custom_call_target="Cholesky" | custom-call | tf_op jit(solution)/shard_map/jit(cholesky)/cholesky | solution.py:316
  300.3 0.7 compare_reduce_fusion.2
  302.3 0.7 fusion.12
  303.1 4.1 while.4
  303.1 0.7 fusion.60
  303.8 1.3 bitcast_dynamic-update-slice_fusion.4
  305.2 0.7 fusion.60
  305.8 1.3 bitcast_dynamic-update-slice_fusion.4
  307.2 20.1 %custom-call.14 = f32[2,128,128]{1,2,0:T(8,128)S(1)} custom-call(f32[2,128,128]{2,1,0:T(8,128)S(1)} %get-tuple-element.25), custom_call_target="InvertDiagBlocksLowerTriangular" | custom-call | tf_op jit(solution)/shard_map/jit(_solve_triangular)/triangular_solve | solution.py:317
  329.0 0.8 copy.96
  330.6 11.7 %cholesky.164 = f32[128,128]{1,0:T(8,128)S(1)} custom-call(f32[128,128]{1,0:T(8,128)S(1)} %cholesky.197), custom_call_target="Cholesky" | custom-call | tf_op jit(solution)/shard_map/jit(cholesky)/cholesky | solution.py:319
  342.4 9.8 %custom-call.15 = f32[1,128,128]{1,2,0:T(8,128)S(1)} custom-call(f32[1,128,128]{2,1,0:T(8,128)S(1)} %get-tuple-element.70), custom_call_target="InvertDiagBlocksLowerTriangular" | custom-call | tf_op jit(solution)/shard_map/jit(cholesky)/cholesky | solution.py:319
  352.9 11.9 %cholesky.181 = f32[128,128]{1,0:T(8,128)S(1)} custom-call(f32[128,128]{1,0:T(8,128)S(1)} %convolution_subtract_fusion.3), custom_call_target="Cholesky" | custom-call | tf_op jit(solution)/shard_map/jit(cholesky)/cholesky | solution.py:319
  364.8 0.7 compare_reduce_fusion.1
  367.3 0.7 fusion.10
  368.0 4.1 while.5
  368.1 0.7 fusion.61
  368.7 1.3 bitcast_dynamic-update-slice_fusion.5
  370.8 1.3 bitcast_dynamic-update-slice_fusion.5
  372.1 19.7 %custom-call.16 = f32[2,128,128]{1,2,0:T(8,128)S(1)} custom-call(f32[2,128,128]{2,1,0:T(8,128)S(1)} %get-tuple-element.26), custom_call_target="InvertDiagBlocksLowerTriangular" | custom-call | tf_op jit(solution)/shard_map/jit(_solve_triangular)/triangular_solve | solution.py:320
  392.4 1.1 maximum_maximum_fusion
  393.5 1.3 copy.95
  394.8 1.1 fusion.2
  397.8 2.8 fusion.39
  400.6 1.1 select_maximum_fusion
  401.7 12.4 %shard_map.55.own_ref = f32[24,2,256,128]{3,2,1,0:T(8,128)} custom-call(s32[64]{0:T(128)S(1)} %select_reduce_fusion.4.order_ref, s32[97]{0:T(128)S(1)} %convert_reduce_fusion.start_ref, s32[3]{0:T(128)S(1)} %pad_add_fusion.where_ref, f32[64,256,128]{2,1,0:T(8,128)} %bitcast.7.arrived_ref, f32[2,256]{1,0:T(2,128)S(1)} %copy-done), custom_call_target="tpu_custom_call" | custom-call | tf_op jit(solution)/shard_map/pallas_call | solution.py:349
  414.2 480.0 %shard_map.56 = (f32[2,24,2,256,128]{4,3,2,1,0:T(8,128)}, f32[2,2,2,256,128]{4,3,2,1,0:T(8,128)}) custom-call(f32[24,2,256,128]{3,2,1,0:T(8,128)} %shard_map.55.own_ref), custom_call_target="tpu_custom_call" | custom-call | tf_op jit(solution)/shard_map/pallas_call | solution.py:365
  894.2 2.0 copy.91
  896.2 0.8 reshape.114
  897.1 3.1 convolution_negate_fusion
  900.2 1.2 slice_select_fusion
  901.5 29.7 %shard_map.57 = f32[24576,128]{1,0:T(8,128)} custom-call(s32[64]{0:T(128)S(1)} %select_reduce_fusion.4.order_ref, s32[97]{0:T(128)S(1)} %convert_reduce_fusion.start_ref, s32[3]{0:T(128)S(1)} %pad_add_fusion.where_ref, f32[64,256,128]{2,1,0:T(8,128)} %bitcast.7.arrived_ref, f32[2,256]{1,0:T(2,128)S(1)} %copy-done, ...), custom_call_target="tpu_custom_call" | custom-call | tf_op jit(solution)/shard_map/pallas_call | solution.py:395
  (81 shorter events, 10.9 us)
Async XLA Ops:
  8.9 17.1 %all-to-all-start = ((s32[32,1,2]{2,1,0:T(1,128)}), s32[32,1,2]{2,1,0:T(1,128)S(1)}, u32[]{:S(2)}, u32[]{:S(2)}) async-start(s32[32,1,2]{2,1,0:T(1,128)} %bitcast.1), calls=%async_computation | async-start | bytes 32768 | tf_op jit(solution)/shard_map/all_to_all | solution.py:288
  26.0 375.7 %all-to-all-start.1 = ((f32[32,2,256,128]{3,2,1,0:T(8,128)}), f32[32,2,256,128]{3,2,1,0:T(8,128)}, u32[]{:S(2)}, u32[]{:S(2)}) async-start(f32[32,2,256,128]{3,2,1,0:T(8,128)} %bitcast.111), calls=%async_computation.1 | async-start | bytes 16777216 | tf_op jit(solution)/shard_map/all_to_all | solution.py:291
  31.9 231.5 %all-reduce.5.cloned.1.call-start = ((), (), s32[]{:S(2)}) async-start(), calls=%async_computation.2 | async-start | bytes 2097152 | tf_op jit(solution)/shard_map/psum | solution.py:304
  38.3 1.9 slice-start
  395.9 5.8 copy-start
Sparse Core Ops, SparseCore 0:
  40.3 223.0 all-reduce.4

commit v2 on v1

--- a/solution.py
+++ b/solution.py
@@ -57,15 +57,10 @@
     row_tiles = own_ref.shape[0]
     per = row_tiles // pieces
     barrier = pltpu.get_barrier_semaphore()
-    for step in (1, -1):
-        inside = (col < n_col - 1) if step == 1 else (col > 0)
-
-        @pl.when(inside)
-        def _():
-            pl.semaphore_signal(
-                barrier, inc=1, device_id={"col": col + step}, device_id_type=MESH
-            )
-
+    for step in (1, n_col - 1):
+        pl.semaphore_signal(
+            barrier, inc=1, device_id={"col": lax.rem(col + step, n_col)}, device_id_type=MESH
+        )
     for shift in range(1, n_row):
         pl.semaphore_signal(
             barrier,
@@ -73,30 +68,26 @@
             device_id={"row": lax.rem(row + shift, n_row)},
             device_id_type=MESH,
         )
-
-    at_end = jnp.logical_or(col == 0, col == n_col - 1)
-
-    @pl.when(at_end)
-    def _():
-        pl.semaphore_wait(barrier, n_row)
-
-    @pl.when(jnp.logical_not(at_end))
-    def _():
-        pl.semaphore_wait(barrier, n_row + 1)
+    pl.semaphore_wait(barrier, n_row + 1)
 
     def part(ref, piece):
         return ref.at[pl.ds(piece * per, per)]
 
-    def hop(section, piece, step, from_own):
+    def distance(section, piece):
+        if piece % 2 == 0:
+            return lax.rem(col - section + n_col, n_col)
+        return lax.rem(section - col + n_col, n_col)
+
+    def hop(section, piece, from_own):
+        step = 1 if piece % 2 == 0 else n_col - 1
         target = all_ref.at[section]
         source = own_ref if from_own else target
-        way = 0 if step == 1 else 1
         return pltpu.make_async_remote_copy(
             src_ref=part(source, piece),
             dst_ref=part(target, piece),
-            send_sem=send_sem.at[section, way, piece],
+            send_sem=send_sem.at[section, piece],
             recv_sem=recv_sem.at[section, piece],
-            device_id={"col": col + step},
+            device_id={"col": lax.rem(col + step, n_col)},
             device_id_type=MESH,
         )
 
@@ -107,11 +98,9 @@
 
         @pl.when(col == section)
         def _():
+            for piece in range(pieces):
+                hop(section, piece, True).start()
             local(section).start()
-            for piece in range(pieces):
-                hop(section, piece, 1, True).start()
-                if section > 0:
-                    hop(section, piece, -1, True).start()
             local(section).wait()
 
     def row_copy(block, section, shift):
@@ -143,19 +132,11 @@
 
             @pl.when(col != section)
             def _():
-                hop(section, piece, 1, False).wait_recv()
-
-            if section < n_col - 1:
-
-                @pl.when(jnp.logical_and(col > section, col < n_col - 1))
-                def _():
-                    hop(section, piece, 1, False).start()
-
-            if section > 1:
-
-                @pl.when(jnp.logical_and(col < section, col > 0))
-                def _():
-                    hop(section, piece, -1, False).start()
+                hop(section, piece, False).wait_recv()
+
+            @pl.when(jnp.logical_and(col != section, distance(section, piece) < n_col - 1))
+            def _():
+                hop(section, piece, False).start()
 
         if piece == send_rows_at:
             for block in range(col_blocks):
@@ -184,15 +165,9 @@
     for section in range(SECTIONS):
         for piece in range(pieces):
 
-            @pl.when(jnp.logical_and(col >= section, col < n_col - 1))
+            @pl.when(distance(section, piece) < n_col - 1)
             def _():
-                hop(section, piece, 1, False).wait_send()
-
-            if section > 0:
-
-                @pl.when(jnp.logical_and(col <= section, col > 0))
-                def _():
-                    hop(section, piece, -1, False).wait_send()
+                hop(section, piece, False).wait_send()
 
 
 def final_kernel(col_blocks, halves, n_col, order_ref, start_ref, where_ref, arrived_ref, diag_ref, panels_ref, whi_ref, wlo_ref, top_ref, own_ref, out_ref, lhs_ref):
@@ -285,6 +260,20 @@
     targets = jnp.sum(hit * (local_tile + 1)[None, :], axis=1, dtype=jnp.int32) - 1
     masked = child_tiles * tile_mask.astype(jnp.float32)[:, :, None]
     outgoing = masked[source]
+    wide = SECTIONS * panel_width
+    in_pivot = is_live & (row_tile < SECTIONS) & (col_tile < (row_tile + 1) * halves)
+    pivot_block = row_tile * (row_tile + 1) // 2 + col_block
+    pivot_count = SECTIONS * (SECTIONS + 1) // 2
+    pivot_slot = jnp.where(in_pivot, pivot_block * halves + col_half, pivot_count * halves)
+    pivot = jax.ops.segment_sum(masked, pivot_slot, num_segments=pivot_count * halves + 1)
+    pivot = pivot[: pivot_count * halves].reshape(pivot_count, halves, tile_rows, tile_cols)
+    pivot = pivot.transpose(0, 2, 1, 3).reshape(pivot_count, tile_rows, panel_width)
+    own_diag = jnp.where(
+        (jnp.arange(pivot_count) == col_index * (col_index + 3) // 2) & (row_index == 0), 1.0, 0.0
+    )
+    pivot = pivot + own_diag[:, None, None] * jnp.diag(front_diagonal[0])[None]
+    pivot = lax.psum(pivot, ("row", "col"))
+    pivot, outgoing = lax.optimization_barrier((pivot, outgoing))
     arrived_targets = lax.all_to_all(
         targets.reshape(devices, CAP), ("row", "col"), split_axis=0, concat_axis=0, tiled=True
     )
@@ -296,21 +285,8 @@
         tiled=True,
     ).reshape(-1, tile_rows, tile_cols)
 
-    wide = SECTIONS * panel_width
-    pivot_tiles = SECTIONS * halves
-    in_pivot = is_live & (row_tile < SECTIONS) & (col_tile < pivot_tiles)
-    pivot_slot = jnp.where(in_pivot, row_tile * pivot_tiles + col_tile, SECTIONS * pivot_tiles)
-    pivot = jax.ops.segment_sum(masked, pivot_slot, num_segments=SECTIONS * pivot_tiles + 1)
-    pivot = lax.psum(pivot[: SECTIONS * pivot_tiles], ("row", "col"))
-    pivot = pivot.reshape(SECTIONS, pivot_tiles, tile_rows, tile_cols)
-    pivot = pivot.transpose(0, 2, 1, 3).reshape(wide, wide)
-    one_col = (jnp.arange(SECTIONS, dtype=jnp.int32) == col_index)[:, None] & (row_index == 0)
-    diag = lax.psum(jnp.where(one_col, front_diagonal[0][None, :], 0.0), ("row", "col"))
-    pivot = pivot + jnp.diag(diag.reshape(-1))
     eye = jnp.eye(panel_width, dtype=jnp.float32)
-    b00 = pivot[:panel_width, :panel_width]
-    b10 = pivot[panel_width:, :panel_width]
-    b11 = pivot[panel_width:, panel_width:]
+    b00, b10, b11 = pivot
     b00 = 0.5 * (b00 + b00.T)
     b11 = 0.5 * (b11 + b11.T)
     l00 = jnp.linalg.cholesky(b00)
@@ -376,7 +352,7 @@
         out_specs=(anywhere, anywhere),
         scratch_shapes=[
             pltpu.SemaphoreType.DMA,
-            pltpu.SemaphoreType.DMA((SECTIONS, 2, pieces)),
+            pltpu.SemaphoreType.DMA((SECTIONS, pieces)),
             pltpu.SemaphoreType.DMA((SECTIONS, pieces)),
             pltpu.SemaphoreType.DMA((col_blocks, SECTIONS, n_row)),
             pltpu.SemaphoreType.DMA((col_blocks, SECTIONS)),

time: 943 us -> 949 us (level)
  blocking collectives: 204 us -> 0 us
  waiting for transfers between devices: 17.5 us -> 156 us
  Pallas kernels: 522 us -> 595 us
    psum x1 -> x0, blocking collectives: 204 us -> none  [on_device(): lax.psum(jnp.where(one_col, front_diagonal[0][None, :], 0.0), ('row', 'co...]
    psum x1, waiting for transfers between devices: 17.5 us -> 116 us  [on_device(): pivot = lax.psum(pivot, ('row', 'col'))]
    pallas_call x1, Pallas kernels: 480 us -> 553 us  [on_device(): pl.pallas_call(functools.partial(chain_kernel, n_row, n_col, col_blocks,...]
    all_to_all x1, waiting for transfers between devices: 0.01 us -> 40.2 us  [on_device(): lax.all_to_all(outgoing.reshape(devices, CAP, tile_rows, tile_cols), ('ro...]
    another operation x6 -> x7, other arithmetic: 34 us -> 34.6 us  [on_device(): l00 = jnp.linalg.cholesky(b00)]
  transfers between devices with their start and end apart: 3 -> 3, of which waited for: 1 -> 2; matrix products, arithmetic and copies ran while one was open for 17% -> 15% of each run, Pallas kernels for 0% -> 0%
where the time goes in v2:
time: 949 us; the launch traced here: 943 us
  Pallas kernels  595 us (63%)
  waiting for transfers between devices  156 us (16%)
  other arithmetic  128 us (13%)
  local copies, waits for them, and re-layouts  23.7 us (2%)
  between operations  17.3 us (2%)
  starting transfers between devices  11.3 us (1%)
  matrix products  11.3 us (1%)
    pallas_call x1, Pallas kernels, on_device(): pl.pallas_call(functools.partial(chain_kernel, n_row, n_col, col_blocks,...  553 us
    psum x1, waiting for transfers between devices, on_device(): pivot = lax.psum(pivot, ('row', 'col'))  116 us
    all_to_all x1, waiting for transfers between devices, on_device(): lax.all_to_all(outgoing.reshape(devices, CAP, tile_rows, tile_cols), ('ro...  40.2 us
    another operation x7, other arithmetic, on_device(): l11 = jnp.linalg.cholesky(b11 - mm(l10, l10.T))  34.8 us
    another operation x7, other arithmetic, on_device(): l00 = jnp.linalg.cholesky(b00)  34.6 us
    pallas_call x1, Pallas kernels, on_device(): pl.pallas_call(functools.partial(final_kernel, col_blocks, halves, n_col)...  29.7 us
    another operation x4, other arithmetic, on_device(): x0 = jax.scipy.linalg.solve_triangular(l00, eye, lower=True)  20.1 us
    another operation x2, other arithmetic, on_device(): x1 = jax.scipy.linalg.solve_triangular(l11, eye, lower=True)  19.7 us
  transfers between devices with their start and end apart: 3, of which 2 were waited for; matrix products, arithmetic and copies ran while one was open for 15% of the time, Pallas kernels for 0%

profile of v2, /device:TPU:24, one launch (start us, length us, event | category | flops | bytes accessed | tf_op | source)
XLA Modules:
  0.0 942.5 jit_solution(16399628362571931629)
XLA Ops:
  7.2 0.7 slice.46
  7.9 0.8 convert_element_type.29
  8.7 0.7 and_select_fusion.2
  9.4 3.9 broadcast_multiply_fusion
  13.4 6.2 scatter_fusion
  19.7 1.0 bitcast_add_fusion
  21.1 0.7 sub.41
  21.8 5.9 all-to-all-start
  27.7 6.5 gather_fusion
  34.3 115.5 %all-reduce.5.cloned.1.call-done = f32[3,256,256]{2,1,0:T(8,128)} async-done(((f32[3,256,256]{2,1,0:T(8,128)}), f32[3,256,256]{2,1,0:T(8,128)}) %all-reduce.5.cloned.1.call-update) | async-done | bytes 786448 | tf_op jit(solution)/shard_map/psum | solution.py:275
  149.8 5.5 all-to-all-start.1
  156.0 0.7 reduce.11
  157.2 0.8 slice_bitcast_fusion.2
  158.0 0.8 copy.94
  159.6 11.7 %cholesky.130 = f32[128,128]{1,0:T(8,128)S(1)} custom-call(f32[128,128]{1,0:T(8,128)S(1)} %copy.78), custom_call_target="Cholesky" | custom-call | tf_op jit(solution)/shard_map/jit(cholesky)/cholesky | solution.py:292
  171.4 9.8 %custom-call.13 = f32[1,128,128]{1,2,0:T(8,128)S(1)} custom-call(f32[1,128,128]{2,1,0:T(8,128)S(1)} %get-tuple-element.78), custom_call_target="InvertDiagBlocksLowerTriangular" | custom-call | tf_op jit(solution)/shard_map/jit(cholesky)/cholesky | solution.py:292
  181.9 11.7 %cholesky.147 = f32[128,128]{1,0:T(8,128)S(1)} custom-call(f32[128,128]{1,0:T(8,128)S(1)} %copy.80), custom_call_target="Cholesky" | custom-call | tf_op jit(solution)/shard_map/jit(cholesky)/cholesky | solution.py:292
  193.6 0.6 compare_reduce_fusion.3
  194.2 0.7 compare_reduce_fusion.2
  196.3 3.8 while.4
  196.9 1.3 bitcast_dynamic-update-slice_fusion.4
  198.8 1.3 bitcast_dynamic-update-slice_fusion.4
  200.1 20.1 %custom-call.14 = f32[2,128,128]{1,2,0:T(8,128)S(1)} custom-call(f32[2,128,128]{2,1,0:T(8,128)S(1)} %get-tuple-element.29), custom_call_target="InvertDiagBlocksLowerTriangular" | custom-call | tf_op jit(solution)/shard_map/jit(_solve_triangular)/triangular_solve | solution.py:293
  220.6 1.2 maximum_maximum_fusion
  221.8 1.3 copy.95
  224.5 0.6 convolution_subtract_fusion
  225.3 11.7 %cholesky.164 = f32[128,128]{1,0:T(8,128)S(1)} custom-call(f32[128,128]{1,0:T(8,128)S(1)} %cholesky.197), custom_call_target="Cholesky" | custom-call | tf_op jit(solution)/shard_map/jit(cholesky)/cholesky | solution.py:295
  237.1 9.8 %custom-call.15 = f32[1,128,128]{1,2,0:T(8,128)S(1)} custom-call(f32[1,128,128]{2,1,0:T(8,128)S(1)} %get-tuple-element.74), custom_call_target="InvertDiagBlocksLowerTriangular" | custom-call | tf_op jit(solution)/shard_map/jit(cholesky)/cholesky | solution.py:295
  247.6 11.9 %cholesky.181 = f32[128,128]{1,0:T(8,128)S(1)} custom-call(f32[128,128]{1,0:T(8,128)S(1)} %convolution_subtract_fusion.3), custom_call_target="Cholesky" | custom-call | tf_op jit(solution)/shard_map/jit(cholesky)/cholesky | solution.py:295
  259.5 0.7 compare_reduce_fusion.1
  260.2 0.6 compare_reduce_fusion
  262.2 4.1 while.5
  262.2 0.7 fusion.58
  262.9 1.3 bitcast_dynamic-update-slice_fusion.5
  264.2 0.7 fusion.58
  264.9 1.3 bitcast_dynamic-update-slice_fusion.5
  266.3 19.7 %custom-call.16 = f32[2,128,128]{1,2,0:T(8,128)S(1)} custom-call(f32[2,128,128]{2,1,0:T(8,128)S(1)} %get-tuple-element.30), custom_call_target="InvertDiagBlocksLowerTriangular" | custom-call | tf_op jit(solution)/shard_map/jit(_solve_triangular)/triangular_solve | solution.py:296
  287.9 0.6 convolution_negate_fusion.1
  288.5 2.8 fusion.37
  291.4 1.1 select_maximum_fusion
  292.5 40.2 %all-to-all-done.1 = f32[32,2,256,128]{3,2,1,0:T(8,128)} async-done(((f32[32,2,256,128]{3,2,1,0:T(8,128)}), f32[32,2,256,128]{3,2,1,0:T(8,128)}, u32[]{:S(2)}, u32[]{:S(2)}) %all-to-all-start.1) | async-done | bytes 8388640 | tf_op jit(solution)/shard_map/all_to_all | solution.py:280
  332.7 12.4 %shard_map.55.own_ref = f32[24,2,256,128]{3,2,1,0:T(8,128)} custom-call(s32[64]{0:T(128)S(1)} %select_reduce_fusion.4.order_ref, s32[97]{0:T(128)S(1)} %convert_reduce_fusion.start_ref, s32[3]{0:T(128)S(1)} %pad_add_fusion.where_ref, f32[64,256,128]{2,1,0:T(8,128)} %bitcast.10.arrived_ref, f32[2,256]{1,0:T(2,128)S(1)} %copy-done), custom_call_target="tpu_custom_call" | custom-call | tf_op jit(solution)/shard_map/pallas_call | solution.py:325
  345.1 553.4 %shard_map.56 = (f32[2,24,2,256,128]{4,3,2,1,0:T(8,128)}, f32[2,2,2,256,128]{4,3,2,1,0:T(8,128)}) custom-call(f32[24,2,256,128]{3,2,1,0:T(8,128)} %shard_map.55.own_ref), custom_call_target="tpu_custom_call" | custom-call | tf_op jit(solution)/shard_map/pallas_call | solution.py:341
  898.5 2.0 copy.91
  900.5 0.8 reshape.133
  901.4 3.1 convolution_negate_fusion
  904.5 1.2 slice_select_fusion
  905.8 29.7 %shard_map.57 = f32[24576,128]{1,0:T(8,128)} custom-call(s32[64]{0:T(128)S(1)} %select_reduce_fusion.4.order_ref, s32[97]{0:T(128)S(1)} %convert_reduce_fusion.start_ref, s32[3]{0:T(128)S(1)} %pad_add_fusion.where_ref, f32[64,256,128]{2,1,0:T(8,128)} %bitcast.10.arrived_ref, f32[2,256]{1,0:T(2,128)S(1)} %copy-done, ...), custom_call_target="tpu_custom_call" | custom-call | tf_op jit(solution)/shard_map/pallas_call | solution.py:371
  (79 shorter events, 9.3 us)
Async XLA Ops:
  6.5 143.2 %all-reduce.5.cloned.1.call-start = ((), (), s32[]{:S(2)}) async-start(), calls=%async_computation.2 | async-start | bytes 1572864 | tf_op jit(solution)/shard_map/psum | solution.py:275
  21.8 128.0 %all-to-all-start = ((s32[32,1,2]{2,1,0:T(1,128)}), s32[32,1,2]{2,1,0:T(1,128)S(1)}, u32[]{:S(2)}, u32[]{:S(2)}) async-start(s32[32,1,2]{2,1,0:T(1,128)} %bitcast.1), calls=%async_computation | async-start | bytes 32768 | tf_op jit(solution)/shard_map/all_to_all | solution.py:277
  149.8 7.4 copy-start.1
  149.8 182.9 %all-to-all-start.1 = ((f32[32,2,256,128]{3,2,1,0:T(8,128)}), f32[32,2,256,128]{3,2,1,0:T(8,128)}, u32[]{:S(2)}, u32[]{:S(2)}) async-start(f32[32,2,256,128]{3,2,1,0:T(8,128)} %bitcast.117), calls=%async_computation.1 | async-start | bytes 16777216 | tf_op jit(solution)/shard_map/all_to_all | solution.py:280
  286.6 46.0 %copy-start = (f32[2,256]{1,0:T(2,128)S(1)}, f32[2,256]{1,0:T(2,128)}, u32[]{:S(2)}) copy-start(f32[2,256]{1,0:T(2,128)} %diag_ref.3) | copy-start | bytes 6148
Sparse Core Ops, SparseCore 0:
  20.9 128.8 all-reduce.4

commit v3 on v1

--- a/solution.py
+++ b/solution.py
@@ -108,10 +108,9 @@
         @pl.when(col == section)
         def _():
             local(section).start()
-            for piece in range(pieces):
-                hop(section, piece, 1, True).start()
-                if section > 0:
-                    hop(section, piece, -1, True).start()
+            if section == 0:
+                for piece in range(pieces):
+                    hop(section, piece, 1, True).start()
             local(section).wait()
 
     def row_copy(block, section, shift):
@@ -138,7 +137,20 @@
 
     needed = min(col_blocks * n_col, row_tiles)
     send_rows_at = -(-needed // per) - 1
+    copies = [(section, shift) for shift in range(1, n_row) for section in range(SECTIONS)]
+    batch = -(-len(copies) // (pieces - send_rows_at))
+    odd = lax.rem(row, 2) == 1
     for piece in range(pieces):
+        for section in range(1, SECTIONS):
+
+            @pl.when(jnp.logical_and(col == section, jnp.logical_not(odd)))
+            def _():
+                hop(section, piece, -1, True).start()
+
+            @pl.when(jnp.logical_and(col == section, col < n_col - 1))
+            def _():
+                hop(section, piece, 1, True).start()
+
         for section in range(SECTIONS):
 
             @pl.when(col != section)
@@ -157,15 +169,23 @@
                 def _():
                     hop(section, piece, -1, False).start()
 
-        if piece == send_rows_at:
+        for section in range(1, SECTIONS):
+
+            @pl.when(jnp.logical_and(col == section, odd))
+            def _():
+                hop(section, piece, -1, True).start()
+
+        if piece >= send_rows_at:
+            low = (piece - send_rows_at) * batch
             for block in range(col_blocks):
 
                 @pl.when(owner(block))
                 def _():
-                    for section in range(SECTIONS):
-                        for shift in range(1, n_row):
-                            row_copy(block, section, shift).start()
-                        row_local(block, section).start()
+                    if piece == send_rows_at:
+                        for section in range(SECTIONS):
+                            row_local(block, section).start()
+                    for section, shift in copies[low : low + batch]:
+                        row_copy(block, section, shift).start()
 
     for block in range(col_blocks):
 
@@ -285,6 +305,20 @@
     targets = jnp.sum(hit * (local_tile + 1)[None, :], axis=1, dtype=jnp.int32) - 1
     masked = child_tiles * tile_mask.astype(jnp.float32)[:, :, None]
     outgoing = masked[source]
+    wide = SECTIONS * panel_width
+    in_pivot = is_live & (row_tile < SECTIONS) & (col_tile < (row_tile + 1) * halves)
+    pivot_block = row_tile * (row_tile + 1) // 2 + col_block
+    pivot_count = SECTIONS * (SECTIONS + 1) // 2
+    pivot_slot = jnp.where(in_pivot, pivot_block * halves + col_half, pivot_count * halves)
+    pivot = jax.ops.segment_sum(masked, pivot_slot, num_segments=pivot_count * halves + 1)
+    pivot = pivot[: pivot_count * halves].reshape(pivot_count, halves, tile_rows, tile_cols)
+    pivot = pivot.transpose(0, 2, 1, 3).reshape(pivot_count, tile_rows, panel_width)
+    own_diag = jnp.where(
+        (jnp.arange(pivot_count) == col_index * (col_index + 3) // 2) & (row_index == 0), 1.0, 0.0
+    )
+    pivot = pivot + own_diag[:, None, None] * jnp.diag(front_diagonal[0])[None]
+    pivot = lax.psum(pivot, ("row", "col"))
+    pivot, outgoing = lax.optimization_barrier((pivot, outgoing))
     arrived_targets = lax.all_to_all(
         targets.reshape(devices, CAP), ("row", "col"), split_axis=0, concat_axis=0, tiled=True
     )
@@ -296,21 +330,8 @@
         tiled=True,
     ).reshape(-1, tile_rows, tile_cols)
 
-    wide = SECTIONS * panel_width
-    pivot_tiles = SECTIONS * halves
-    in_pivot = is_live & (row_tile < SECTIONS) & (col_tile < pivot_tiles)
-    pivot_slot = jnp.where(in_pivot, row_tile * pivot_tiles + col_tile, SECTIONS * pivot_tiles)
-    pivot = jax.ops.segment_sum(masked, pivot_slot, num_segments=SECTIONS * pivot_tiles + 1)
-    pivot = lax.psum(pivot[: SECTIONS * pivot_tiles], ("row", "col"))
-    pivot = pivot.reshape(SECTIONS, pivot_tiles, tile_rows, tile_cols)
-    pivot = pivot.transpose(0, 2, 1, 3).reshape(wide, wide)
-    one_col = (jnp.arange(SECTIONS, dtype=jnp.int32) == col_index)[:, None] & (row_index == 0)
-    diag = lax.psum(jnp.where(one_col, front_diagonal[0][None, :], 0.0), ("row", "col"))
-    pivot = pivot + jnp.diag(diag.reshape(-1))
     eye = jnp.eye(panel_width, dtype=jnp.float32)
-    b00 = pivot[:panel_width, :panel_width]
-    b10 = pivot[panel_width:, :panel_width]
-    b11 = pivot[panel_width:, panel_width:]
+    b00, b10, b11 = pivot
     b00 = 0.5 * (b00 + b00.T)
     b11 = 0.5 * (b11 + b11.T)
     l00 = jnp.linalg.cholesky(b00)

time: 943 us -> 893 us (0.947)
  blocking collectives: 204 us -> 0 us
  waiting for transfers between devices: 17.5 us -> 156 us
  Pallas kernels: 522 us -> 541 us
    psum x1 -> x0, blocking collectives: 204 us -> none  [on_device(): lax.psum(jnp.where(one_col, front_diagonal[0][None, :], 0.0), ('row', 'co...]
    psum x1, waiting for transfers between devices: 17.5 us -> 115 us  [on_device(): pivot = lax.psum(pivot, ('row', 'col'))]
    all_to_all x1, waiting for transfers between devices: 0.01 us -> 40.2 us  [on_device(): lax.all_to_all(outgoing.reshape(devices, CAP, tile_rows, tile_cols), ('ro...]
    pallas_call x1, Pallas kernels: 480 us -> 499 us  [on_device(): pl.pallas_call(functools.partial(chain_kernel, n_row, n_col, col_blocks,...]
    another operation x6 -> x7, other arithmetic: 34 us -> 34.6 us  [on_device(): l00 = jnp.linalg.cholesky(b00)]
  transfers between devices with their start and end apart: 3 -> 3, of which waited for: 1 -> 2; matrix products, arithmetic and copies ran while one was open for 17% -> 16% of each run, Pallas kernels for 0% -> 0%
where the time goes in v3:
time: 893 us; the launch traced here: 888 us
  Pallas kernels  541 us (61%)
  waiting for transfers between devices  156 us (17%)
  other arithmetic  128 us (14%)
  local copies, waits for them, and re-layouts  23.7 us (3%)
  between operations  17.3 us (2%)
  starting transfers between devices  11.3 us (1%)
  matrix products  11.3 us (1%)
    pallas_call x1, Pallas kernels, on_device(): pl.pallas_call(functools.partial(chain_kernel, n_row, n_col, col_blocks,...  499 us
    psum x1, waiting for transfers between devices, on_device(): pivot = lax.psum(pivot, ('row', 'col'))  115 us
    all_to_all x1, waiting for transfers between devices, on_device(): lax.all_to_all(outgoing.reshape(devices, CAP, tile_rows, tile_cols), ('ro...  40.2 us
    another operation x7, other arithmetic, on_device(): l11 = jnp.linalg.cholesky(b11 - mm(l10, l10.T))  35 us
    another operation x7, other arithmetic, on_device(): l00 = jnp.linalg.cholesky(b00)  34.6 us
    pallas_call x1, Pallas kernels, on_device(): pl.pallas_call(functools.partial(final_kernel, col_blocks, halves, n_col)...  29.7 us
    another operation x4, other arithmetic, on_device(): x0 = jax.scipy.linalg.solve_triangular(l00, eye, lower=True)  19.9 us
    another operation x2, other arithmetic, on_device(): x1 = jax.scipy.linalg.solve_triangular(l11, eye, lower=True)  19.7 us
  transfers between devices with their start and end apart: 3, of which 2 were waited for; matrix products, arithmetic and copies ran while one was open for 16% of the time, Pallas kernels for 0%

profile of v3, /device:TPU:24, one launch (start us, length us, event | category | flops | bytes accessed | tf_op | source)
XLA Modules:
  0.0 888.4 jit_solution(2094164109403288350)
XLA Ops:
  7.2 0.7 slice.46
  7.9 0.8 convert_element_type.29
  8.7 0.7 and_select_fusion.2
  9.4 3.9 broadcast_multiply_fusion
  13.4 6.2 scatter_fusion
  19.7 1.0 bitcast_add_fusion
  21.1 0.7 sub.41
  21.8 5.9 all-to-all-start
  27.7 6.5 gather_fusion
  34.3 115.5 %all-reduce.5.cloned.1.call-done = f32[3,256,256]{2,1,0:T(8,128)} async-done(((f32[3,256,256]{2,1,0:T(8,128)}), f32[3,256,256]{2,1,0:T(8,128)}) %all-reduce.5.cloned.1.call-update) | async-done | bytes 786448 | tf_op jit(solution)/shard_map/psum | solution.py:320
  149.7 5.4 all-to-all-start.1
  155.9 0.7 reduce.11
  157.2 0.8 slice_bitcast_fusion.2
  158.0 0.8 copy.94
  159.6 11.7 %cholesky.130 = f32[128,128]{1,0:T(8,128)S(1)} custom-call(f32[128,128]{1,0:T(8,128)S(1)} %copy.78), custom_call_target="Cholesky" | custom-call | tf_op jit(solution)/shard_map/jit(cholesky)/cholesky | solution.py:337
  171.3 9.8 %custom-call.13 = f32[1,128,128]{1,2,0:T(8,128)S(1)} custom-call(f32[1,128,128]{2,1,0:T(8,128)S(1)} %get-tuple-element.78), custom_call_target="InvertDiagBlocksLowerTriangular" | custom-call | tf_op jit(solution)/shard_map/jit(cholesky)/cholesky | solution.py:337
  181.8 11.7 %cholesky.147 = f32[128,128]{1,0:T(8,128)S(1)} custom-call(f32[128,128]{1,0:T(8,128)S(1)} %copy.80), custom_call_target="Cholesky" | custom-call | tf_op jit(solution)/shard_map/jit(cholesky)/cholesky | solution.py:337
  193.5 0.6 compare_reduce_fusion.3
  194.2 0.7 compare_reduce_fusion.2
  196.2 3.8 while.4
  196.9 1.3 bitcast_dynamic-update-slice_fusion.4
  198.8 1.3 bitcast_dynamic-update-slice_fusion.4
  200.1 19.9 %custom-call.14 = f32[2,128,128]{1,2,0:T(8,128)S(1)} custom-call(f32[2,128,128]{2,1,0:T(8,128)S(1)} %get-tuple-element.29), custom_call_target="InvertDiagBlocksLowerTriangular" | custom-call | tf_op jit(solution)/shard_map/jit(_solve_triangular)/triangular_solve | solution.py:338
  220.4 1.2 maximum_maximum_fusion
  221.6 1.3 copy.95
  224.3 0.6 convolution_subtract_fusion
  225.1 11.7 %cholesky.164 = f32[128,128]{1,0:T(8,128)S(1)} custom-call(f32[128,128]{1,0:T(8,128)S(1)} %cholesky.197), custom_call_target="Cholesky" | custom-call | tf_op jit(solution)/shard_map/jit(cholesky)/cholesky | solution.py:340
  236.8 9.8 %custom-call.15 = f32[1,128,128]{1,2,0:T(8,128)S(1)} custom-call(f32[1,128,128]{2,1,0:T(8,128)S(1)} %get-tuple-element.74), custom_call_target="InvertDiagBlocksLowerTriangular" | custom-call | tf_op jit(solution)/shard_map/jit(cholesky)/cholesky | solution.py:340
  247.3 12.1 %cholesky.181 = f32[128,128]{1,0:T(8,128)S(1)} custom-call(f32[128,128]{1,0:T(8,128)S(1)} %convolution_subtract_fusion.3), custom_call_target="Cholesky" | custom-call | tf_op jit(solution)/shard_map/jit(cholesky)/cholesky | solution.py:340
  259.5 0.7 compare_reduce_fusion.1
  260.2 0.6 compare_reduce_fusion
  262.2 4.1 while.5
  262.2 0.7 fusion.58
  262.9 1.3 bitcast_dynamic-update-slice_fusion.5
  264.2 0.7 fusion.58
  264.9 1.3 bitcast_dynamic-update-slice_fusion.5
  266.3 19.7 %custom-call.16 = f32[2,128,128]{1,2,0:T(8,128)S(1)} custom-call(f32[2,128,128]{2,1,0:T(8,128)S(1)} %get-tuple-element.30), custom_call_target="InvertDiagBlocksLowerTriangular" | custom-call | tf_op jit(solution)/shard_map/jit(_solve_triangular)/triangular_solve | solution.py:341
  287.9 0.6 convolution_negate_fusion.1
  288.5 2.8 fusion.37
  291.3 1.1 select_maximum_fusion
  292.5 40.2 %all-to-all-done.1 = f32[32,2,256,128]{3,2,1,0:T(8,128)} async-done(((f32[32,2,256,128]{3,2,1,0:T(8,128)}), f32[32,2,256,128]{3,2,1,0:T(8,128)}, u32[]{:S(2)}, u32[]{:S(2)}) %all-to-all-start.1) | async-done | bytes 8388640 | tf_op jit(solution)/shard_map/all_to_all | solution.py:325
  332.6 12.4 %shard_map.55.own_ref = f32[24,2,256,128]{3,2,1,0:T(8,128)} custom-call(s32[64]{0:T(128)S(1)} %select_reduce_fusion.4.order_ref, s32[97]{0:T(128)S(1)} %convert_reduce_fusion.start_ref, s32[3]{0:T(128)S(1)} %pad_add_fusion.where_ref, f32[64,256,128]{2,1,0:T(8,128)} %bitcast.10.arrived_ref, f32[2,256]{1,0:T(2,128)S(1)} %copy-done), custom_call_target="tpu_custom_call" | custom-call | tf_op jit(solution)/shard_map/pallas_call | solution.py:370
  345.1 499.3 %shard_map.56 = (f32[2,24,2,256,128]{4,3,2,1,0:T(8,128)}, f32[2,2,2,256,128]{4,3,2,1,0:T(8,128)}) custom-call(f32[24,2,256,128]{3,2,1,0:T(8,128)} %shard_map.55.own_ref), custom_call_target="tpu_custom_call" | custom-call | tf_op jit(solution)/shard_map/pallas_call | solution.py:386
  844.4 2.0 copy.91
  846.4 0.8 reshape.133
  847.3 3.1 convolution_negate_fusion
  850.4 1.2 slice_select_fusion
  851.7 29.7 %shard_map.57 = f32[24576,128]{1,0:T(8,128)} custom-call(s32[64]{0:T(128)S(1)} %select_reduce_fusion.4.order_ref, s32[97]{0:T(128)S(1)} %convert_reduce_fusion.start_ref, s32[3]{0:T(128)S(1)} %pad_add_fusion.where_ref, f32[64,256,128]{2,1,0:T(8,128)} %bitcast.10.arrived_ref, f32[2,256]{1,0:T(2,128)S(1)} %copy-done, ...), custom_call_target="tpu_custom_call" | custom-call | tf_op jit(solution)/shard_map/pallas_call | solution.py:416
  (79 shorter events, 9.3 us)
Async XLA Ops:
  6.5 143.2 %all-reduce.5.cloned.1.call-start = ((), (), s32[]{:S(2)}) async-start(), calls=%async_computation.2 | async-start | bytes 1572864 | tf_op jit(solution)/shard_map/psum | solution.py:320
  21.8 127.9 %all-to-all-start = ((s32[32,1,2]{2,1,0:T(1,128)}), s32[32,1,2]{2,1,0:T(1,128)S(1)}, u32[]{:S(2)}, u32[]{:S(2)}) async-start(s32[32,1,2]{2,1,0:T(1,128)} %bitcast.1), calls=%async_computation | async-start | bytes 32768 | tf_op jit(solution)/shard_map/all_to_all | solution.py:322
  149.7 7.4 copy-start.1
  149.7 182.9 %all-to-all-start.1 = ((f32[32,2,256,128]{3,2,1,0:T(8,128)}), f32[32,2,256,128]{3,2,1,0:T(8,128)}, u32[]{:S(2)}, u32[]{:S(2)}) async-start(f32[32,2,256,128]{3,2,1,0:T(8,128)} %bitcast.117), calls=%async_computation.1 | async-start | bytes 16777216 | tf_op jit(solution)/shard_map/all_to_all | solution.py:325
  286.6 46.0 %copy-start = (f32[2,256]{1,0:T(2,128)S(1)}, f32[2,256]{1,0:T(2,128)}, u32[]{:S(2)}) copy-start(f32[2,256]{1,0:T(2,128)} %diag_ref.3) | copy-start | bytes 6148
Sparse Core Ops, SparseCore 0:
  20.9 128.8 all-reduce.4
